TPU v7x, 32 devices: a whole 2x2x4 slice. The times are simulated.
32 devices in a mesh: row: 4 (over y, core), col: 8 (over z, x).
Axes of the slice: x: 2, y: 2, z: 4, core: 2. Of those that a mesh axis runs over, the one named last changes fastest.
Arguments:
- left: bfloat16 [8, 16, 512, 256], P('row', 'col'), may hold values from -0.11767578 to 0.11767578
- right: bfloat16 [8, 16, 512, 256], P('row', 'col'), may hold values from -6 to 6
- lower_inverse: bfloat16 [2, 512, 512], P(None, 'row'), as said below
- upper_inverse: bfloat16 [2, 512, 512], P(None, None, 'col'), as said below
- ranks: int32 [8, 16], P('row', 'col'), may hold values from 16 to 256, as said below
Outputs:
- right_out: bfloat16 [8, 16, 512, 256], P('row', 'col')
Inputs may be any that keep to these rules, and one draw needn't show every extreme that they name: Tile ranks: every row of `ranks` contains at least one entry equal to 256; all entries lie in 4..256. Each lower_inverse[k] is lower triangular with a positive diagonal. Each upper_inverse[k] is upper triangular with a positive diagonal.
All inputs are finite; a program needn't handle non-finite values.
Results may differ from a plain program's by a relative error of at most 0.009.
Values may be sent and summed in bfloat16 or wider, within the bound.
A program may use at most 64 MiB of HBM per device.

v0:
```python
import jax
import jax.numpy as jnp
from jax import lax
from jax.sharding import PartitionSpec as P


def broadcast(value, axis, source):
    kept = jnp.where(lax.axis_index(axis) == source, value, 0).astype(value.dtype)
    return lax.psum(kept, axis)


def update_tiles(
    left, right, col_left, col_right, row_left, row_right, tile_rows, tile_cols, panel
):
    core = jnp.einsum("abr,cbs->acrs", col_right, row_left, preferred_element_type=jnp.float32)
    intersection = jnp.einsum("acbr,abs->acrs", left, col_left, preferred_element_type=jnp.float32)
    mixed = jnp.einsum(
        "acrs,acst->acrt", intersection, core, precision=lax.Precision.HIGHEST
    ).astype(jnp.bfloat16)
    change = jnp.einsum("cbt,acrt->acbr", row_right, mixed, preferred_element_type=jnp.float32)
    fresh = (right.astype(jnp.float32) - change).astype(jnp.bfloat16)
    below = (tile_rows > panel)[:, None, None, None]
    trail = below & (tile_cols > panel)[None, :, None, None]
    on_panel = below & (tile_cols == panel)[None, :, None, None]
    kept = jnp.where(on_panel, col_right[:, None], right)
    return jnp.where(trail, fresh, kept)


def body(left, right, lower_inverse, upper_inverse, ranks):
    slots = lax.broadcasted_iota(jnp.int32, ranks.shape + (left.shape[3],), 2)
    keep = (slots < ranks[:, :, None]).astype(jnp.bfloat16)
    left = left * keep[:, :, None, :]
    right = right * keep[:, :, None, :]
    row_count = lax.axis_size("row")
    col_count = lax.axis_size("col")
    row_index = lax.axis_index("row")
    col_index = lax.axis_index("col")
    tile_rows = jnp.arange(left.shape[0], dtype=jnp.int32) * row_count + row_index
    tile_cols = jnp.arange(left.shape[1], dtype=jnp.int32) * col_count + col_index
    full_lower = lax.all_gather(lower_inverse, "row", axis=1, tiled=True)
    full_upper = lax.all_gather(upper_inverse, "col", axis=2, tiled=True)
    for panel in range(lower_inverse.shape[0]):

        def solve_column(factor):
            return jnp.einsum(
                "bc,abr->acr", full_upper[panel], factor, preferred_element_type=jnp.float32
            ).astype(jnp.bfloat16)

        def solve_row(factor):
            return jnp.einsum(
                "cb,jbr->jcr", full_lower[panel], factor, preferred_element_type=jnp.float32
            ).astype(jnp.bfloat16)

        solved_col = lax.cond(col_index == panel, solve_column, lambda factor: factor, right[:, 0])
        col_left, col_right = (
            broadcast(left[:, 0], "col", panel),
            broadcast(solved_col, "col", panel),
        )
        solved_row = lax.cond(row_index == panel, solve_row, lambda factor: factor, left[0])
        row_left, row_right = (
            broadcast(solved_row, "row", panel),
            broadcast(right[0], "row", panel),
        )
        right = update_tiles(
            left, right, col_left, col_right, row_left, row_right, tile_rows, tile_cols, panel
        )
    return right


def solution(mesh):
    placed = (
        P("row", "col", None, None),
        P("row", "col", None, None),
        P(None, "row", None),
        P(None, None, "col"),
        P("row", "col"),
    )
    return jax.shard_map(
        body, mesh=mesh, in_specs=placed, out_specs=P("row", "col", None, None), check_vma=False
    )
```

profile of v0, /device:TPU:28, one launch (start us, length us, event | category | flops | bytes accessed | tf_op | source)
XLA Modules:
  0.0 325.1 jit_solution(1950935950600516134)
XLA Ops:
  6.5 1.7 copy.21
  9.8 1.7 broadcast_multiply_fusion
  11.5 1.2 select_bitcast_fusion
  12.7 36.6 %all-gather.5.cloned.1.call-done = bf16[2,512,512]{1,0,2:T(2,128)(2,1)} async-done(((bf16[2,512,64]{1,0,2:T(2,128)(2,1)}), bf16[2,512,512]{1,0,2:T(2,128)(2,1)}) %all-gather.5.cloned.1.call-update) | async-done | bytes 1048592 | tf_op jit(solution)/shard_map/all_gather | solution.py:41
  49.6 0.9 broadcast_select_fusion.2
  50.8 0.9 fusion.17
  51.7 15.1 %all-gather.3.cloned.1.call-done = bf16[2,512,512]{2,1,0:T(8,128)(2,1)} async-done(((bf16[2,128,512]{2,1,0:T(8,128)(2,1)}), bf16[2,512,512]{2,1,0:T(8,128)(2,1)}) %all-gather.3.cloned.1.call-update) | async-done | bytes 1048592 | tf_op jit(solution)/shard_map/all_gather | solution.py:40
  67.8 80.6 %all-reduce.11.cloned.1.call-done = (bf16[2,512,256]{1,2,0:T(8,128)(2,1)}, bf16[2,512,256]{2,1,0:T(8,128)(2,1)}) async-done(((bf16[2,512,256]{1,2,0:T(8,128)(2,1)}, bf16[2,512,256]{2,1,0:T(8,128)(2,1)}), (bf16[2,512,256]{1,2,0:T(8,128)(2,1)}, bf16[2,512,256]{2,1,0:T(8,128)(2,1)})) %all-reduce.11.cloned.1.call-update) | async-done | bytes 1048592 | tf_op jit(solution)/shard_map/psum | solution.py:9
  148.4 2.1 copy.26
  150.5 1.6 fusion.24
  152.1 35.1 %all-reduce.15.cloned.1.call-done = (bf16[2,512,256]{2,1,0:T(8,128)(2,1)}, bf16[2,512,256]{1,2,0:T(8,128)(2,1)}) async-done(((bf16[2,512,256]{2,1,0:T(8,128)(2,1)}, bf16[2,512,256]{1,2,0:T(8,128)(2,1)}), (bf16[2,512,256]{2,1,0:T(8,128)(2,1)}, bf16[2,512,256]{1,2,0:T(8,128)(2,1)})) %all-reduce.15.cloned.1.call-update) | async-done | bytes 1048592 | tf_op jit(solution)/shard_map/psum | solution.py:9
  187.1 1.7 fusion.22
  189.6 1.2 convolution_convert_fusion.5
  192.6 0.9 copy-done
  193.6 1.3 conditional.7
  193.6 1.3 copy.53
  195.8 0.8 broadcast_select_fusion.1
  197.2 0.9 fusion.16
  198.1 76.0 %all-reduce.9.cloned.1.call-done = (bf16[2,512,256]{1,2,0:T(8,128)(2,1)}, bf16[2,512,256]{2,1,0:T(8,128)(2,1)}) async-done(((bf16[2,512,256]{1,2,0:T(8,128)(2,1)}, bf16[2,512,256]{2,1,0:T(8,128)(2,1)}), (bf16[2,512,256]{1,2,0:T(8,128)(2,1)}, bf16[2,512,256]{2,1,0:T(8,128)(2,1)})) %all-reduce.9.cloned.1.call-update) | async-done | bytes 1048592 | tf_op jit(solution)/shard_map/psum | solution.py:9
  274.1 2.1 copy.33
  276.7 36.0 %all-reduce.13.cloned.1.call-done = (bf16[2,512,256]{2,1,0:T(8,128)(2,1)}, bf16[2,512,256]{1,2,0:T(8,128)(2,1)}) async-done(((bf16[2,512,256]{2,1,0:T(8,128)(2,1)}, bf16[2,512,256]{1,2,0:T(8,128)(2,1)}), (bf16[2,512,256]{2,1,0:T(8,128)(2,1)}, bf16[2,512,256]{1,2,0:T(8,128)(2,1)})) %all-reduce.13.cloned.1.call-update) | async-done | bytes 1048592 | tf_op jit(solution)/shard_map/psum | solution.py:9
  312.8 1.5 fusion.18
  315.2 1.2 convolution_convert_fusion.4
  316.6 1.6 fusion.11
  (56 shorter events, 9.2 us)
Async XLA Ops:
  6.5 42.8 %all-gather.5.cloned.1.call-start = ((), (), s32[]{:S(2)}) async-start(), calls=%async_computation.1 | async-start | bytes 1179648 | tf_op jit(solution)/shard_map/all_gather | solution.py:41
  8.3 58.5 %all-gather.3.cloned.1.call-start = ((), (), s32[]{:S(2)}) async-start(), calls=%async_computation | async-start | bytes 1310720 | tf_op jit(solution)/shard_map/all_gather | solution.py:40
  9.0 139.4 %all-reduce.11.cloned.1.call-start = ((), (), s32[]{:S(2)}) async-start(), calls=%async_computation.3 | async-start | bytes 2097152 | tf_op jit(solution)/shard_map/psum | solution.py:9
  11.5 39.3 %copy-start.1 = (bf16[2,2,512,256]{3,2,1,0:T(8,128)(2,1)}, bf16[2,2,512,256]{3,2,1,0:T(8,128)(2,1)S(1)}, u32[]{:S(2)}) copy-start(bf16[2,2,512,256]{3,2,1,0:T(8,128)(2,1)S(1)} %get-tuple-element.76) | copy-start | bytes 3145732
  50.5 136.7 %all-reduce.15.cloned.1.call-start = ((), (), s32[]{:S(2)}) async-start(), calls=%async_computation.5 | async-start | bytes 2097152 | tf_op jit(solution)/shard_map/psum | solution.py:9
  67.7 206.4 %all-reduce.9.cloned.1.call-start = ((), (), s32[]{:S(2)}) async-start(), calls=%async_computation.2 | async-start | bytes 2097152 | tf_op jit(solution)/shard_map/psum | solution.py:9
  189.6 1.2 copy-start.2
  189.6 1.3 copy-start.9
  189.6 1.5 copy-start.10
  191.7 1.8 copy-start.4
  191.8 1.8 copy-start
  195.7 117.1 %all-reduce.13.cloned.1.call-start = ((), (), s32[]{:S(2)}) async-start(), calls=%async_computation.4 | async-start | bytes 2097152 | tf_op jit(solution)/shard_map/psum | solution.py:9
  195.8 1.4 copy-start.5
  274.1 2.1 copy-start.7
  276.2 36.6 %copy-start.3 = (bf16[2,512,256]{1,2,0:T(8,128)(2,1)S(1)}, bf16[2,512,256]{1,2,0:T(8,128)(2,1)}, u32[]{:S(2)}) copy-start(bf16[2,512,256]{1,2,0:T(8,128)(2,1)} %get-tuple-element.65) | copy-start | bytes 1572868
  315.1 1.2 copy-start.6
  315.1 1.3 copy-start.8
  315.1 1.5 copy-start.11
Sparse Core Ops, SparseCore 0:
  9.5 39.8 all-gather.4
  50.9 15.7 all-gather.2
  70.3 78.0 all-reduce.10
  150.9 36.1 all-reduce.14
  195.8 78.2 all-reduce.8
  276.5 36.1 all-reduce.12
where the time goes:
time: 328 us; the launch traced here: 325 us
  waiting for transfers between devices  280 us (85%)
  between operations  13.7 us (4%)
  local copies, waits for them, and re-layouts  12.2 us (4%)
  matrix products  9.76 us (3%)
  other arithmetic  8.93 us (3%)
    psum x4, waiting for transfers between devices, broadcast(): return lax.psum(kept, axis)  228 us
    all_gather x1, waiting for transfers between devices, body(): full_upper = lax.all_gather(upper_inverse, 'col', axis=2, tiled=True)  36.6 us
    all_gather x1, waiting for transfers between devices, body(): full_lower = lax.all_gather(lower_inverse, 'row', axis=1, tiled=True)  15.1 us
  transfers between devices with their start and end apart: 6, of which 6 were waited for; matrix products, arithmetic and copies ran while one was open for 5% of the time, Pallas kernels for 0%

commit v1 on v0

v1 whole, which is shorter than its diff:
```python
import functools

import jax
import jax.numpy as jnp
from jax import lax
from jax.experimental import pallas as pl
from jax.experimental.pallas import tpu as pltpu
from jax.sharding import PartitionSpec as P

CHUNKS = 4
MESH = pl.DeviceIdType.MESH


def matmul(a, b):
    return jnp.dot(a, b, preferred_element_type=jnp.float32)


def matmul_tn(a, b):
    return lax.dot_general(a, b, (((0,), (0,)), ((), ())), preferred_element_type=jnp.float32)


def matmul_nt(a, b):
    return lax.dot_general(a, b, (((1,), (1,)), ((), ())), preferred_element_type=jnp.float32)


def children(index, extent, minor, source):
    x, m = lax.rem(index, minor), lax.div(index, minor)
    found = [((x == source) & (m + 1 < extent // minor), index + minor)]
    if source + 1 < minor:
        found.append(((x >= source) & (x + 1 < minor), index + 1))
    if source > 0:
        found.append(((x <= source) & (x >= 1), index - 1))
    return found


def kernel(
    n_row, n_col, minor_col, ranks, left, right, lower, upper, out,
    ul, col_u, col_y, row_y, row_u, low, up,
    send_sem, recv_sem, inv_send, low_recv, up_recv,
):
    r, c = lax.axis_index("row"), lax.axis_index("col")
    order, width = left.shape[2], left.shape[3]
    step = order // CHUNKS
    barrier = pltpu.get_barrier_semaphore()
    for d in range(1, n_row):
        pl.semaphore_signal(
            barrier, inc=1, device_id={"row": lax.rem(r + d, n_row)}, device_id_type=MESH
        )
    for d in range(1, n_col):
        pl.semaphore_signal(
            barrier, inc=1, device_id={"col": lax.rem(c + d, n_col)}, device_id_type=MESH
        )

    lanes = lax.broadcasted_iota(jnp.int32, (1, width), 1)

    def keep(a, b):
        return (lanes < ranks[a, b]).astype(jnp.float32).astype(jnp.bfloat16)

    for a in range(2):
        for b in range(2):
            mask = keep(a, b)
            ul[a, b] = left[a, b] * mask
            out[a, b] = right[a, b] * mask
    for k in range(2):

        @pl.when(c == k)
        def _():
            up[pl.ds(k * upper.shape[1], upper.shape[1])] = upper[k]
            for a in range(2):
                col_u[k, a] = ul[a, 0]

        @pl.when(r == k)
        def _():
            low[pl.ds(k * lower.shape[1], lower.shape[1])] = lower[k]
            if k == 0:
                for b in range(2):
                    row_y[0, b] = out[0, b]

    pl.semaphore_wait(barrier, n_row - 1 + n_col - 1)

    buffers = {"cu": col_u, "cy": col_y, "ru": row_u, "ry": row_y}
    place = {
        (kind, k, t): n
        for n, (kind, k, t) in enumerate(
            (kind, k, t) for kind in ("cu", "cy", "ru", "ry") for k in range(2) for t in range(2)
        )
    }
    started = []

    def axis_of(item):
        return "col" if item[0][0] == "c" else "row"

    def tree(item):
        if axis_of(item) == "col":
            return children(c, n_col, minor_col, item[1])
        return children(r, n_row, 2, item[1])

    def copy_of(item, chunk, way, target):
        kind, k, t = item
        view = buffers[kind].at[k, t, pl.ds(chunk * step, step)]
        return pltpu.make_async_remote_copy(
            src_ref=view,
            dst_ref=view,
            send_sem=send_sem.at[place[item], chunk, way],
            recv_sem=recv_sem.at[place[item], chunk],
            device_id={axis_of(item): target},
            device_id_type=MESH,
        )

    def push(item, chunk):
        for way, (needed, target) in enumerate(tree(item)):

            @pl.when(needed)
            def _():
                copy_of(item, chunk, way, target).start()

        started.append((item, chunk))

    def is_source(item):
        return (c if axis_of(item) == "col" else r) == item[1]

    def send(item):
        @pl.when(is_source(item))
        def _():
            for chunk in range(CHUNKS):
                for way, (needed, target) in enumerate(tree(item)):

                    @pl.when(needed)
                    def _():
                        copy_of(item, chunk, way, target).start()

    def relay(items):
        for chunk in range(CHUNKS):
            for item in items:

                @pl.when(jnp.logical_not(is_source(item)))
                def _():
                    copy_of(item, chunk, 0, 0).wait_recv()
                    for way, (needed, target) in enumerate(tree(item)):

                        @pl.when(needed)
                        def _():
                            copy_of(item, chunk, way, target).start()

    def up_copy(k, source):
        rows = upper.shape[1]
        return pltpu.make_async_remote_copy(
            src_ref=upper.at[k],
            dst_ref=up.at[pl.ds(pl.multiple_of(source * rows, rows), rows)],
            send_sem=inv_send.at[0, k],
            recv_sem=up_recv.at[source],
            device_id={"col": k},
            device_id_type=MESH,
        )

    def low_copy(k, source):
        rows = lower.shape[1]
        return pltpu.make_async_remote_copy(
            src_ref=lower.at[k],
            dst_ref=low.at[pl.ds(pl.multiple_of(source * rows, rows), rows)],
            send_sem=inv_send.at[1, k],
            recv_sem=low_recv.at[source],
            device_id={"row": k},
            device_id_type=MESH,
        )

    for k in range(2):

        @pl.when(c != k)
        def _():
            up_copy(k, c).start()

        @pl.when(r != k)
        def _():
            low_copy(k, r).start()

    send(("cu", 0, 0))
    send(("cu", 1, 0))
    for b in range(2):
        send(("ry", 0, b))

    @pl.when(c < 2)
    def _():
        for s in range(n_col):

            @pl.when(s != c)
            def _():
                up_copy(0, s).wait_recv()

    @pl.when(c == 0)
    def _():
        col_y[0, 0] = matmul(up[...], out[0, 0]).astype(jnp.bfloat16)

    send(("cy", 0, 0))
    send(("cu", 0, 1))
    send(("cu", 1, 1))

    @pl.when(c == 0)
    def _():
        col_y[0, 1] = matmul(up[...], out[1, 0]).astype(jnp.bfloat16)

    send(("cy", 0, 1))

    @pl.when(r < 2)
    def _():
        for s in range(n_row):

            @pl.when(s != r)
            def _():
                low_copy(0, s).wait_recv()

    for b in range(2):
        for k in range(2):

            @pl.when(r == k)
            def _():
                row_u[k, b] = matmul(low[...], ul[0, b]).astype(jnp.bfloat16)

            send(("ru", k, b))

    def update(panel, a):
        row_in = (a * n_row + r) > panel
        for b in range(2):
            tile_col = b * n_col + c

            @pl.when(row_in & (tile_col > panel))
            def _():
                core = matmul_tn(col_y[panel, a], row_u[panel, b]).astype(jnp.bfloat16)
                meet = matmul_tn(ul[a, b], col_u[panel, a]).astype(jnp.bfloat16)
                mixed = matmul(meet, core).astype(jnp.bfloat16)
                change = matmul_nt(row_y[panel, b], mixed)
                out[a, b] = (out[a, b].astype(jnp.float32) - change).astype(jnp.bfloat16)

        @pl.when(row_in & (c == panel))
        def _():
            out[a, 0] = col_y[panel, a]

    def solve_next(a):
        @pl.when(c == 1)
        def _():
            col_y[1, a] = matmul(up[...], out[a, 0]).astype(jnp.bfloat16)

        send(("cy", 1, a))

    relay([("cu", 0, 0), ("cu", 1, 0), ("ry", 0, 0), ("ry", 0, 1)])
    relay([("cy", 0, 0), ("ru", 0, 0), ("ru", 0, 1)])
    update(0, 0)
    solve_next(0)

    @pl.when(r == 1)
    def _():
        for b in range(2):
            row_y[1, b] = out[0, b]

    for b in range(2):
        send(("ry", 1, b))
    relay([("cu", 0, 1), ("cu", 1, 1), ("ru", 1, 0)])
    relay([("cy", 0, 1), ("ru", 1, 1)])
    update(0, 1)
    solve_next(1)
    relay([("cy", 1, 0), ("ry", 1, 0), ("ry", 1, 1)])
    update(1, 0)
    relay([("cy", 1, 1)])
    update(1, 1)

    for k in range(2):

        @pl.when(c != k)
        def _():
            up_copy(k, c).wait_send()

        @pl.when(r != k)
        def _():
            low_copy(k, r).wait_send()

    for item in place:
        for way, (needed, target) in enumerate(tree(item)):

            @pl.when(needed)
            def _():
                for chunk in range(CHUNKS):
                    copy_of(item, chunk, way, target).wait_send()


def body(left, right, lower_inverse, upper_inverse, ranks):
    n_row, n_col = lax.axis_size("row"), lax.axis_size("col")
    minor_col = 4 if n_col % 4 == 0 and n_col > 8 else 2
    order, width = left.shape[2:]
    upper = jnp.swapaxes(upper_inverse, 1, 2)
    tile = (order, width)
    vmem = pl.BlockSpec(memory_space=pltpu.VMEM)
    return pl.pallas_call(
        functools.partial(kernel, n_row, n_col, minor_col),
        out_shape=jax.ShapeDtypeStruct(right.shape, jnp.bfloat16),
        in_specs=[pl.BlockSpec(memory_space=pltpu.SMEM)] + [vmem] * 4,
        out_specs=vmem,
        scratch_shapes=[
            pltpu.VMEM((2, 2) + tile, jnp.bfloat16),
            pltpu.VMEM((2, 2) + tile, jnp.bfloat16),
            pltpu.VMEM((2, 2) + tile, jnp.bfloat16),
            pltpu.VMEM((2, 2) + tile, jnp.bfloat16),
            pltpu.VMEM((2, 2) + tile, jnp.bfloat16),
            pltpu.VMEM((order, order), jnp.bfloat16),
            pltpu.VMEM((order, order), jnp.bfloat16),
            pltpu.SemaphoreType.DMA((16, CHUNKS, 3)),
            pltpu.SemaphoreType.DMA((16, CHUNKS)),
            pltpu.SemaphoreType.DMA((2, 2)),
            pltpu.SemaphoreType.DMA((n_row,)),
            pltpu.SemaphoreType.DMA((n_col,)),
        ],
        compiler_params=pltpu.CompilerParams(
            collective_id=0, has_side_effects=True, vmem_limit_bytes=40 * 1024 * 1024
        ),
        cost_estimate=pl.CostEstimate(
            flops=2_000_000_000, bytes_accessed=4_000_000, transcendentals=0
        ),
    )(ranks, left, right, lower_inverse, upper)


def solution(mesh):
    placed = (
        P("row", "col", None, None),
        P("row", "col", None, None),
        P(None, "row", None),
        P(None, None, "col"),
        P("row", "col"),
    )
    return jax.shard_map(
        body, mesh=mesh, in_specs=placed, out_specs=P("row", "col", None, None), check_vma=False
    )
```

time: 328 us -> 103 us (0.31)
  waiting for transfers between devices: 280 us -> 0 us
  Pallas kernels: 0 us -> 96.5 us
  between operations: 13.7 us -> 0.01 us
  matrix products: 9.76 us -> 0 us
  other arithmetic: 8.93 us -> 0 us
  local copies, waits for them, and re-layouts: 12.2 us -> 5.95 us
    psum x4 -> x0, waiting for transfers between devices: 228 us -> none  [broadcast(): return lax.psum(kept, axis)]
    pallas_call x0 -> x1, Pallas kernels: none -> 96.5 us  [body(): pl.pallas_call(functools.partial(kernel, n_row, n_col, minor_col), out_sh...]
    all_gather x2 -> x0, waiting for transfers between devices: 51.7 us -> none  [the longest x1 36.6 us: body(): full_upper = lax.all_gather(upper_inverse, 'col', axis=2, tiled=True)]
    dot_general x8 -> x0, matrix products: 9.76 us -> none  [the longest x2 3.17 us: update_tiles(): jnp.einsum('abr,cbs->acrs', col_right, row_left, preferred_element_type=j...]
    select_n x7 -> x0, other arithmetic: 6.31 us -> none  [broadcast(): jnp.where(lax.axis_index(axis) == source, value, 0).astype(value.dtype)]
    psum x2 -> x0, local copies, waits for them, and re-layouts: 4.16 us -> none  [broadcast(): return lax.psum(kept, axis)]
  transfers between devices with their start and end apart: 6 -> 0, of which waited for: 6 -> 0; matrix products, arithmetic and copies ran while one was open for 5% -> 0% of each run, Pallas kernels for 0% -> 0%
where the time goes in v1:
time: 103 us; the launch traced here: 102 us
  Pallas kernels  96.5 us (94%)
  local copies, waits for them, and re-layouts  5.95 us (6%)
    pallas_call x1, Pallas kernels, body(): pl.pallas_call(functools.partial(kernel, n_row, n_col, minor_col), out_sh...  96.5 us
    unnamed x11, local copies, waits for them, and re-layouts  5.95 us

profile of v1, /device:TPU:28, one launch (start us, length us, event | category | flops | bytes accessed | tf_op | source)
XLA Modules:
  0.0 102.4 jit_solution(66801588971561185)
XLA Ops:
  0.0 0.0 copy-start.4
  0.0 0.7 copy-done.4
  0.7 0.0 copy-start
  0.7 1.2 %copy-done = bf16[2,2,512,256]{3,2,1,0:T(8,128)(2,1)S(1)} copy-done((bf16[2,2,512,256]{3,2,1,0:T(8,128)(2,1)S(1)}, bf16[2,2,512,256]{3,2,1,0:T(8,128)(2,1)}, u32[]{:S(2)}) %copy-start) | copy-done | bytes 1048600
  1.9 0.0 copy-start.1
  1.9 1.2 %copy-done.1 = bf16[2,2,512,256]{3,2,1,0:T(8,128)(2,1)S(1)} copy-done((bf16[2,2,512,256]{3,2,1,0:T(8,128)(2,1)S(1)}, bf16[2,2,512,256]{3,2,1,0:T(8,128)(2,1)}, u32[]{:S(2)}) %copy-start.1) | copy-done | bytes 1048600
  3.1 0.0 copy-start.2
  3.1 0.9 copy-done.2
  4.1 0.0 copy-start.3
  4.1 0.9 copy-done.3
  5.0 96.5 %shard_map.55 = bf16[2,2,512,256]{3,2,1,0:T(8,128)(2,1)S(1)} custom-call(s32[2,2]{1,0:T(2,128)S(1)} %copy-done.4, bf16[2,2,512,256]{3,2,1,0:T(8,128)(2,1)S(1)} %copy-done, bf16[2,2,512,256]{3,2,1,0:T(8,128)(2,1)S(1)} %copy-done.1, bf16[2,128,512]{2,1,0:T(8,128)(2,1)S(1)} %copy-done.2, bf16[2,64,512]{2,1,0:T(8,128)(2,1)S(1)} %bitcast.1), custom_call_target="tpu_custom_call" | custom-call | flops 2000000000 | bytes 4000000 | tf_op jit(solution)/shard_map/pallas_call | solution.py:292
  101.5 1.0 copy.7
Async XLA Ops:
  0.0 0.7 copy-start.4
  0.7 1.2 %copy-start = (bf16[2,2,512,256]{3,2,1,0:T(8,128)(2,1)S(1)}, bf16[2,2,512,256]{3,2,1,0:T(8,128)(2,1)}, u32[]{:S(2)}) copy-start(bf16[2,2,512,256]{3,2,1,0:T(8,128)(2,1)} %left.1) | copy-start | bytes 3145732
  1.9 1.2 %copy-start.1 = (bf16[2,2,512,256]{3,2,1,0:T(8,128)(2,1)S(1)}, bf16[2,2,512,256]{3,2,1,0:T(8,128)(2,1)}, u32[]{:S(2)}) copy-start(bf16[2,2,512,256]{3,2,1,0:T(8,128)(2,1)} %right.1) | copy-start | bytes 3145732
  3.1 0.9 copy-start.2
  4.1 0.9 copy-start.3

commit v2 on v1

--- a/solution.py
+++ b/solution.py
@@ -36,11 +36,24 @@
 def kernel(
     n_row, n_col, minor_col, ranks, left, right, lower, upper, out,
     ul, col_u, col_y, row_y, row_u, low, up,
-    send_sem, recv_sem, inv_send, low_recv, up_recv,
+    send_sem, recv_sem, inv_send, low_recv, up_recv, fetch_sem,
 ):
     r, c = lax.axis_index("row"), lax.axis_index("col")
     order, width = left.shape[2], left.shape[3]
     step = order // CHUNKS
+    fetch_left = [
+        [pltpu.make_async_copy(left.at[a, b], ul.at[a, b], fetch_sem.at[0, a, b]) for b in range(2)]
+        for a in range(2)
+    ]
+    fetch_right = [
+        [pltpu.make_async_copy(right.at[a, b], out.at[a, b], fetch_sem.at[1, a, b]) for b in range(2)]
+        for a in range(2)
+    ]
+    every = [(a, b) for b in range(2) for a in range(2)]
+    for a, b in every:
+        fetch_left[a][b].start()
+        fetch_right[a][b].start()
+
     barrier = pltpu.get_barrier_semaphore()
     for d in range(1, n_row):
         pl.semaphore_signal(
@@ -51,30 +64,48 @@
             barrier, inc=1, device_id={"col": lax.rem(c + d, n_col)}, device_id_type=MESH
         )
 
+    own_rows = {"up": upper.shape[1], "low": lower.shape[1]}
+
+    def own_up(k):
+        rows = own_rows["up"]
+        return pltpu.make_async_copy(upper.at[k], up.at[pl.ds(k * rows, rows)], inv_send.at[0, k])
+
+    def own_low(k):
+        rows = own_rows["low"]
+        return pltpu.make_async_copy(lower.at[k], low.at[pl.ds(k * rows, rows)], inv_send.at[1, k])
+
+    for k in range(2):
+
+        @pl.when(c == k)
+        def _():
+            own_up(k).start()
+
+        @pl.when(r == k)
+        def _():
+            own_low(k).start()
+
     lanes = lax.broadcasted_iota(jnp.int32, (1, width), 1)
 
     def keep(a, b):
         return (lanes < ranks[a, b]).astype(jnp.float32).astype(jnp.bfloat16)
 
-    for a in range(2):
-        for b in range(2):
-            mask = keep(a, b)
-            ul[a, b] = left[a, b] * mask
-            out[a, b] = right[a, b] * mask
+    for a, b in every:
+        mask = keep(a, b)
+        fetch_left[a][b].wait()
+        ul[a, b] = ul[a, b] * mask
+        fetch_right[a][b].wait()
+        out[a, b] = out[a, b] * mask
     for k in range(2):
 
         @pl.when(c == k)
         def _():
-            up[pl.ds(k * upper.shape[1], upper.shape[1])] = upper[k]
             for a in range(2):
                 col_u[k, a] = ul[a, 0]
 
-        @pl.when(r == k)
-        def _():
-            low[pl.ds(k * lower.shape[1], lower.shape[1])] = lower[k]
-            if k == 0:
-                for b in range(2):
-                    row_y[0, b] = out[0, b]
+    @pl.when(r == 0)
+    def _():
+        for b in range(2):
+            row_y[0, b] = out[0, b]
 
     pl.semaphore_wait(barrier, n_row - 1 + n_col - 1)
 
@@ -85,7 +116,6 @@
             (kind, k, t) for kind in ("cu", "cy", "ru", "ry") for k in range(2) for t in range(2)
         )
     }
-    started = []
 
     def axis_of(item):
         return "col" if item[0][0] == "c" else "row"
@@ -107,40 +137,48 @@
             device_id_type=MESH,
         )
 
-    def push(item, chunk):
-        for way, (needed, target) in enumerate(tree(item)):
-
-            @pl.when(needed)
-            def _():
-                copy_of(item, chunk, way, target).start()
-
-        started.append((item, chunk))
+    def wanted(item):
+        kind, k, t = item
+        if t > 0:
+            return True
+        return (r if axis_of(item) == "col" else c) > k
 
     def is_source(item):
         return (c if axis_of(item) == "col" else r) == item[1]
 
+    def is_main(item):
+        if axis_of(item) == "col":
+            return lax.rem(c, minor_col) == item[1]
+        return lax.rem(r, 2) == item[1]
+
+    def forward(item, chunk):
+        for way, (needed, target) in enumerate(tree(item)):
+
+            @pl.when(needed)
+            def _():
+                copy_of(item, chunk, way, target).start()
+
     def send(item):
-        @pl.when(is_source(item))
+        @pl.when(is_source(item) & wanted(item))
         def _():
             for chunk in range(CHUNKS):
-                for way, (needed, target) in enumerate(tree(item)):
-
-                    @pl.when(needed)
-                    def _():
-                        copy_of(item, chunk, way, target).start()
-
-    def relay(items):
+                forward(item, chunk)
+
+    def relay(items, also=True):
         for chunk in range(CHUNKS):
-            for item in items:
-
-                @pl.when(jnp.logical_not(is_source(item)))
+            for item, main in items:
+                role = is_main(item) if main else jnp.logical_not(is_main(item))
+
+                @pl.when(jnp.logical_not(is_source(item)) & wanted(item) & role & also)
                 def _():
                     copy_of(item, chunk, 0, 0).wait_recv()
-                    for way, (needed, target) in enumerate(tree(item)):
-
-                        @pl.when(needed)
-                        def _():
-                            copy_of(item, chunk, way, target).start()
+                    forward(item, chunk)
+
+    def main(*items):
+        relay([(item, True) for item in items])
+
+    def leaf(*items, also=True):
+        relay([(item, False) for item in items], also)
 
     def up_copy(k, source):
         rows = upper.shape[1]
@@ -179,6 +217,16 @@
     for b in range(2):
         send(("ry", 0, b))
 
+    for k in range(2):
+
+        @pl.when(c == k)
+        def _():
+            own_up(k).wait()
+
+        @pl.when(r == k)
+        def _():
+            own_low(k).wait()
+
     @pl.when(c < 2)
     def _():
         for s in range(n_col):
@@ -218,22 +266,23 @@
 
             send(("ru", k, b))
 
-    def update(panel, a):
+    def update(panel, a, b, also=True):
         row_in = (a * n_row + r) > panel
-        for b in range(2):
-            tile_col = b * n_col + c
-
-            @pl.when(row_in & (tile_col > panel))
-            def _():
-                core = matmul_tn(col_y[panel, a], row_u[panel, b]).astype(jnp.bfloat16)
-                meet = matmul_tn(ul[a, b], col_u[panel, a]).astype(jnp.bfloat16)
-                mixed = matmul(meet, core).astype(jnp.bfloat16)
-                change = matmul_nt(row_y[panel, b], mixed)
-                out[a, b] = (out[a, b].astype(jnp.float32) - change).astype(jnp.bfloat16)
-
-        @pl.when(row_in & (c == panel))
-        def _():
-            out[a, 0] = col_y[panel, a]
+        tile_col = b * n_col + c
+
+        @pl.when(row_in & (tile_col > panel) & also)
+        def _():
+            core = matmul_tn(col_y[panel, a], row_u[panel, b]).astype(jnp.bfloat16)
+            meet = matmul_tn(ul[a, b], col_u[panel, a]).astype(jnp.bfloat16)
+            mixed = matmul(meet, core).astype(jnp.bfloat16)
+            change = matmul_nt(row_y[panel, b], mixed)
+            out[a, b] = (out[a, b].astype(jnp.float32) - change).astype(jnp.bfloat16)
+
+        if b == 0:
+
+            @pl.when(row_in & (c == panel) & also)
+            def _():
+                out[a, 0] = col_y[panel, a]
 
     def solve_next(a):
         @pl.when(c == 1)
@@ -242,26 +291,40 @@
 
         send(("cy", 1, a))
 
-    relay([("cu", 0, 0), ("cu", 1, 0), ("ry", 0, 0), ("ry", 0, 1)])
-    relay([("cy", 0, 0), ("ru", 0, 0), ("ru", 0, 1)])
-    update(0, 0)
+    def share_row(b):
+        @pl.when(r == 1)
+        def _():
+            row_y[1, b] = out[0, b]
+
+        send(("ry", 1, b))
+
+    main(("cu", 0, 0), ("cu", 1, 0), ("ry", 0, 0), ("ru", 1, 0))
+    main(("cy", 0, 0), ("cu", 1, 1), ("ru", 0, 0), ("ru", 1, 1))
+    leaf(("cu", 0, 0), ("ry", 0, 0))
+    leaf(("cy", 0, 0), ("ru", 0, 0))
+    update(0, 0, 0)
     solve_next(0)
-
-    @pl.when(r == 1)
-    def _():
-        for b in range(2):
-            row_y[1, b] = out[0, b]
-
-    for b in range(2):
-        send(("ry", 1, b))
-    relay([("cu", 0, 1), ("cu", 1, 1), ("ru", 1, 0)])
-    relay([("cy", 0, 1), ("ru", 1, 1)])
-    update(0, 1)
+    share_row(0)
+    leaf(("ry", 0, 1), ("ru", 0, 1), also=r == 1)
+    update(0, 0, 1, also=r == 1)
+    share_row(1)
+    main(("cu", 0, 1), ("cy", 1, 0), ("ry", 0, 1), ("ry", 1, 0))
+    main(("cy", 0, 1), ("ru", 0, 1), ("ry", 1, 1))
+    leaf(("cu", 0, 1))
+    leaf(("cy", 0, 1))
+    update(0, 1, 0)
     solve_next(1)
-    relay([("cy", 1, 0), ("ry", 1, 0), ("ry", 1, 1)])
-    update(1, 0)
-    relay([("cy", 1, 1)])
-    update(1, 1)
+    leaf(("ry", 0, 1), ("ru", 0, 1), also=r != 1)
+    update(0, 0, 1, also=r != 1)
+    update(0, 1, 1)
+    main(("cy", 1, 1))
+    leaf(("cu", 1, 0), ("cy", 1, 0), ("ru", 1, 0), ("ry", 1, 0))
+    update(1, 0, 0)
+    leaf(("ru", 1, 1), ("ry", 1, 1), ("cu", 1, 1))
+    update(1, 0, 1)
+    leaf(("cy", 1, 1))
+    update(1, 1, 0)
+    update(1, 1, 1)
 
     for k in range(2):
 
@@ -276,7 +339,7 @@
     for item in place:
         for way, (needed, target) in enumerate(tree(item)):
 
-            @pl.when(needed)
+            @pl.when(needed & wanted(item))
             def _():
                 for chunk in range(CHUNKS):
                     copy_of(item, chunk, way, target).wait_send()
@@ -289,10 +352,11 @@
     upper = jnp.swapaxes(upper_inverse, 1, 2)
     tile = (order, width)
     vmem = pl.BlockSpec(memory_space=pltpu.VMEM)
+    hbm = pl.BlockSpec(memory_space=pltpu.HBM)
     return pl.pallas_call(
         functools.partial(kernel, n_row, n_col, minor_col),
         out_shape=jax.ShapeDtypeStruct(right.shape, jnp.bfloat16),
-        in_specs=[pl.BlockSpec(memory_space=pltpu.SMEM)] + [vmem] * 4,
+        in_specs=[pl.BlockSpec(memory_space=pltpu.SMEM)] + [hbm] * 4,
         out_specs=vmem,
         scratch_shapes=[
             pltpu.VMEM((2, 2) + tile, jnp.bfloat16),
@@ -307,6 +371,7 @@
             pltpu.SemaphoreType.DMA((2, 2)),
             pltpu.SemaphoreType.DMA((n_row,)),
             pltpu.SemaphoreType.DMA((n_col,)),
+            pltpu.SemaphoreType.DMA((2, 2, 2)),
         ],
         compiler_params=pltpu.CompilerParams(
             collective_id=0, has_side_effects=True, vmem_limit_bytes=40 * 1024 * 1024

time: 103 us -> 63.2 us (0.61)
  Pallas kernels: 96.5 us -> 57 us
    pallas_call x1, Pallas kernels: 96.5 us -> 57 us  [body(): pl.pallas_call(functools.partial(kernel, n_row, n_col, minor_col), out_sh...]
where the time goes in v2:
time: 63.2 us; the launch traced here: 63 us
  Pallas kernels  57 us (90%)
  local copies, waits for them, and re-layouts  5.95 us (9%)
    pallas_call x1, Pallas kernels, body(): pl.pallas_call(functools.partial(kernel, n_row, n_col, minor_col), out_sh...  57 us
    unnamed x11, local copies, waits for them, and re-layouts  5.95 us

profile of v2, /device:TPU:28, one launch (start us, length us, event | category | flops | bytes accessed | tf_op | source)
XLA Modules:
  0.0 63.0 jit_solution(8928140988504746062)
XLA Ops:
  0.0 0.0 copy-start.4
  0.0 0.7 %copy-done.4 = s32[2,2]{1,0:T(2,128)S(1)} copy-done((s32[2,2]{1,0:T(2,128)S(1)}, s32[2,2]{1,0:T(2,128)}, u32[]{:S(2)}) %copy-start.4) | copy-done | bytes 40
  0.7 0.0 copy-start
  0.7 1.2 %copy-done = bf16[2,2,512,256]{3,2,1,0:T(8,128)(2,1)S(1)} copy-done((bf16[2,2,512,256]{3,2,1,0:T(8,128)(2,1)S(1)}, bf16[2,2,512,256]{3,2,1,0:T(8,128)(2,1)}, u32[]{:S(2)}) %copy-start) | copy-done | bytes 1048600
  1.9 0.0 copy-start.1
  1.9 1.2 %copy-done.1 = bf16[2,2,512,256]{3,2,1,0:T(8,128)(2,1)S(1)} copy-done((bf16[2,2,512,256]{3,2,1,0:T(8,128)(2,1)S(1)}, bf16[2,2,512,256]{3,2,1,0:T(8,128)(2,1)}, u32[]{:S(2)}) %copy-start.1) | copy-done | bytes 1048600
  3.1 0.0 copy-start.2
  3.1 0.9 %copy-done.2 = bf16[2,128,512]{2,1,0:T(8,128)(2,1)S(1)} copy-done((bf16[2,128,512]{2,1,0:T(8,128)(2,1)S(1)}, bf16[2,128,512]{2,1,0:T(8,128)(2,1)}, u32[]{:S(2)}) %copy-start.2) | copy-done | bytes 262168
  4.1 0.0 copy-start.3
  4.1 0.9 %copy-done.3 = bf16[2,512,64]{1,2,0:T(8,128)(2,1)S(1)} copy-done((bf16[2,512,64]{1,2,0:T(8,128)(2,1)S(1)}, bf16[2,512,64]{1,2,0:T(8,128)(2,1)}, u32[]{:S(2)}) %copy-start.3) | copy-done | bytes 131096
  5.0 57.0 %shard_map.55 = bf16[2,2,512,256]{3,2,1,0:T(8,128)(2,1)S(1)} custom-call(s32[2,2]{1,0:T(2,128)S(1)} %copy-done.4, bf16[2,2,512,256]{3,2,1,0:T(8,128)(2,1)S(1)} %copy-done, bf16[2,2,512,256]{3,2,1,0:T(8,128)(2,1)S(1)} %copy-done.1, bf16[2,128,512]{2,1,0:T(8,128)(2,1)S(1)} %copy-done.2, bf16[2,64,512]{2,1,0:T(8,128)(2,1)S(1)} %bitcast.1), custom_call_target="tpu_custom_call" | custom-call | flops 2000000000 | bytes 4000000 | tf_op jit(solution)/shard_map/pallas_call | solution.py:356
  62.0 1.0 %copy.7 = bf16[2,2,512,256]{3,2,1,0:T(8,128)(2,1)} copy(bf16[2,2,512,256]{3,2,1,0:T(8,128)(2,1)S(1)} %shard_map.55) | data formatting | bytes 2097152
Async XLA Ops:
  0.0 0.7 %copy-start.4 = (s32[2,2]{1,0:T(2,128)S(1)}, s32[2,2]{1,0:T(2,128)}, u32[]{:S(2)}) copy-start(s32[2,2]{1,0:T(2,128)} %ranks.1) | copy-start | bytes 52
  0.7 1.2 %copy-start = (bf16[2,2,512,256]{3,2,1,0:T(8,128)(2,1)S(1)}, bf16[2,2,512,256]{3,2,1,0:T(8,128)(2,1)}, u32[]{:S(2)}) copy-start(bf16[2,2,512,256]{3,2,1,0:T(8,128)(2,1)} %left.1) | copy-start | bytes 3145732
  1.9 1.2 %copy-start.1 = (bf16[2,2,512,256]{3,2,1,0:T(8,128)(2,1)S(1)}, bf16[2,2,512,256]{3,2,1,0:T(8,128)(2,1)}, u32[]{:S(2)}) copy-start(bf16[2,2,512,256]{3,2,1,0:T(8,128)(2,1)} %right.1) | copy-start | bytes 3145732
  3.1 0.9 %copy-start.2 = (bf16[2,128,512]{2,1,0:T(8,128)(2,1)S(1)}, bf16[2,128,512]{2,1,0:T(8,128)(2,1)}, u32[]{:S(2)}) copy-start(bf16[2,128,512]{2,1,0:T(8,128)(2,1)} %lower.1) | copy-start | bytes 786436
  4.1 0.9 %copy-start.3 = (bf16[2,512,64]{1,2,0:T(8,128)(2,1)S(1)}, bf16[2,512,64]{1,2,0:T(8,128)(2,1)}, u32[]{:S(2)}) copy-start(bf16[2,512,64]{1,2,0:T(8,128)(2,1)} %param.8) | copy-start | bytes 393220

commit v3 on v2

--- a/solution.py
+++ b/solution.py
@@ -36,7 +36,7 @@
 def kernel(
     n_row, n_col, minor_col, ranks, left, right, lower, upper, out,
     ul, col_u, col_y, row_y, row_u, low, up,
-    send_sem, recv_sem, inv_send, low_recv, up_recv, fetch_sem,
+    send_sem, recv_sem, inv_send, low_recv, up_recv, fetch_sem, swap_sem,
 ):
     r, c = lax.axis_index("row"), lax.axis_index("col")
     order, width = left.shape[2], left.shape[3]
@@ -49,9 +49,10 @@
         [pltpu.make_async_copy(right.at[a, b], out.at[a, b], fetch_sem.at[1, a, b]) for b in range(2)]
         for a in range(2)
     ]
-    every = [(a, b) for b in range(2) for a in range(2)]
+    every = [(1, 0), (0, 0), (0, 1), (1, 1)]
     for a, b in every:
         fetch_left[a][b].start()
+    for a, b in every:
         fetch_right[a][b].start()
 
     barrier = pltpu.get_barrier_semaphore()
@@ -68,7 +69,10 @@
 
     def own_up(k):
         rows = own_rows["up"]
-        return pltpu.make_async_copy(upper.at[k], up.at[pl.ds(k * rows, rows)], inv_send.at[0, k])
+        half = pl.ds(pl.multiple_of(lax.rem(r, 2) * (order // 2), order // 2), order // 2)
+        return pltpu.make_async_copy(
+            upper.at[k, :, half], up.at[pl.ds(k * rows, rows), half], inv_send.at[0, k]
+        )
 
     def own_low(k):
         rows = own_rows["low"]
@@ -88,26 +92,6 @@
 
     def keep(a, b):
         return (lanes < ranks[a, b]).astype(jnp.float32).astype(jnp.bfloat16)
-
-    for a, b in every:
-        mask = keep(a, b)
-        fetch_left[a][b].wait()
-        ul[a, b] = ul[a, b] * mask
-        fetch_right[a][b].wait()
-        out[a, b] = out[a, b] * mask
-    for k in range(2):
-
-        @pl.when(c == k)
-        def _():
-            for a in range(2):
-                col_u[k, a] = ul[a, 0]
-
-    @pl.when(r == 0)
-    def _():
-        for b in range(2):
-            row_y[0, b] = out[0, b]
-
-    pl.semaphore_wait(barrier, n_row - 1 + n_col - 1)
 
     buffers = {"cu": col_u, "cy": col_y, "ru": row_u, "ry": row_y}
     place = {
@@ -158,8 +142,8 @@
             def _():
                 copy_of(item, chunk, way, target).start()
 
-    def send(item):
-        @pl.when(is_source(item) & wanted(item))
+    def send(item, also=True):
+        @pl.when(is_source(item) & wanted(item) & also)
         def _():
             for chunk in range(CHUNKS):
                 forward(item, chunk)
@@ -174,17 +158,30 @@
                     copy_of(item, chunk, 0, 0).wait_recv()
                     forward(item, chunk)
 
-    def main(*items):
-        relay([(item, True) for item in items])
+    def main(*items, also=True):
+        relay([(item, True) for item in items], also)
 
     def leaf(*items, also=True):
         relay([(item, False) for item in items], also)
+
+    half = order // 2
+    mine = pl.ds(pl.multiple_of(lax.rem(r, 2) * half, half), half)
+
+    def swap_halves():
+        return pltpu.make_async_remote_copy(
+            src_ref=up.at[:, mine],
+            dst_ref=up.at[:, mine],
+            send_sem=swap_sem.at[0],
+            recv_sem=swap_sem.at[1],
+            device_id={"row": r + 1 - 2 * lax.rem(r, 2)},
+            device_id_type=MESH,
+        )
 
     def up_copy(k, source):
         rows = upper.shape[1]
         return pltpu.make_async_remote_copy(
-            src_ref=upper.at[k],
-            dst_ref=up.at[pl.ds(pl.multiple_of(source * rows, rows), rows)],
+            src_ref=upper.at[k, :, mine],
+            dst_ref=up.at[pl.ds(pl.multiple_of(source * rows, rows), rows), mine],
             send_sem=inv_send.at[0, k],
             recv_sem=up_recv.at[source],
             device_id={"col": k},
@@ -202,6 +199,17 @@
             device_id_type=MESH,
         )
 
+    for a in range(2):
+        fetch_left[a][0].wait()
+        ul[a, 0] = ul[a, 0] * keep(a, 0)
+        for k in range(2):
+
+            @pl.when(c == k)
+            def _():
+                col_u[k, a] = ul[a, 0]
+
+    pl.semaphore_wait(barrier, n_row - 1 + n_col - 1)
+
     for k in range(2):
 
         @pl.when(c != k)
@@ -213,9 +221,22 @@
             low_copy(k, r).start()
 
     send(("cu", 0, 0))
+    send(("cu", 0, 1), also=r >= 2)
     send(("cu", 1, 0))
-    for b in range(2):
-        send(("ry", 0, b))
+    send(("cu", 1, 1))
+    for a, b in ((0, 0), (0, 1), (1, 0), (1, 1)):
+        fetch_right[a][b].wait()
+        out[a, b] = out[a, b] * keep(a, b)
+        if a == 0:
+
+            @pl.when(r == 0)
+            def _():
+                row_y[0, b] = out[0, b]
+
+            send(("ry", 0, b))
+    for a, b in ((0, 1), (1, 1)):
+        fetch_left[a][b].wait()
+        ul[a, b] = ul[a, b] * keep(a, b)
 
     for k in range(2):
 
@@ -235,13 +256,15 @@
             def _():
                 up_copy(0, s).wait_recv()
 
+        swap_halves().start()
+        swap_halves().wait_recv()
+
     @pl.when(c == 0)
     def _():
         col_y[0, 0] = matmul(up[...], out[0, 0]).astype(jnp.bfloat16)
 
     send(("cy", 0, 0))
-    send(("cu", 0, 1))
-    send(("cu", 1, 1))
+    send(("cu", 0, 1), also=r < 2)
 
     @pl.when(c == 0)
     def _():
@@ -298,18 +321,21 @@
 
         send(("ry", 1, b))
 
-    main(("cu", 0, 0), ("cu", 1, 0), ("ry", 0, 0), ("ru", 1, 0))
-    main(("cy", 0, 0), ("cu", 1, 1), ("ru", 0, 0), ("ru", 1, 1))
-    leaf(("cu", 0, 0), ("ry", 0, 0))
-    leaf(("cy", 0, 0), ("ru", 0, 0))
-    update(0, 0, 0)
-    solve_next(0)
+    main(("cu", 0, 0), ("cu", 1, 0), ("ry", 0, 0))
+    main(("cy", 0, 0), also=r < 2)
+    leaf(("cu", 0, 0), ("ry", 0, 0), ("cy", 0, 0), ("ru", 0, 0), also=r == 1)
+    update(0, 0, 0, also=r == 1)
     share_row(0)
     leaf(("ry", 0, 1), ("ru", 0, 1), also=r == 1)
     update(0, 0, 1, also=r == 1)
     share_row(1)
-    main(("cu", 0, 1), ("cy", 1, 0), ("ry", 0, 1), ("ry", 1, 0))
-    main(("cy", 0, 1), ("ru", 0, 1), ("ry", 1, 1))
+    main(("cu", 0, 1), ("cu", 1, 1), ("ry", 0, 1))
+    main(("cy", 0, 0), ("ru", 0, 0), also=r >= 2)
+    main(("ru", 1, 0))
+    leaf(("cu", 0, 0), ("ry", 0, 0), ("cy", 0, 0), ("ru", 0, 0), also=r != 1)
+    update(0, 0, 0, also=r != 1)
+    solve_next(0)
+    main(("cy", 0, 1), ("cy", 1, 0), ("ru", 0, 1), ("ru", 1, 1))
     leaf(("cu", 0, 1))
     leaf(("cy", 0, 1))
     update(0, 1, 0)
@@ -317,7 +343,8 @@
     leaf(("ry", 0, 1), ("ru", 0, 1), also=r != 1)
     update(0, 0, 1, also=r != 1)
     update(0, 1, 1)
-    main(("cy", 1, 1))
+    main(("cy", 1, 1), ("ry", 1, 0))
+    main(("ry", 1, 1))
     leaf(("cu", 1, 0), ("cy", 1, 0), ("ru", 1, 0), ("ry", 1, 0))
     update(1, 0, 0)
     leaf(("ru", 1, 1), ("ry", 1, 1), ("cu", 1, 1))
@@ -335,6 +362,10 @@
         @pl.when(r != k)
         def _():
             low_copy(k, r).wait_send()
+
+    @pl.when(c < 2)
+    def _():
+        swap_halves().wait_send()
 
     for item in place:
         for way, (needed, target) in enumerate(tree(item)):
@@ -372,9 +403,10 @@
             pltpu.SemaphoreType.DMA((n_row,)),
             pltpu.SemaphoreType.DMA((n_col,)),
             pltpu.SemaphoreType.DMA((2, 2, 2)),
+            pltpu.SemaphoreType.DMA((2,)),
         ],
         compiler_params=pltpu.CompilerParams(
-            collective_id=0, has_side_effects=True, vmem_limit_bytes=40 * 1024 * 1024
+            collective_id=0, has_side_effects=True, vmem_limit_bytes=60 * 1024 * 1024
         ),
         cost_estimate=pl.CostEstimate(
             flops=2_000_000_000, bytes_accessed=4_000_000, transcendentals=0

time: 63.2 us -> 57.4 us (0.908)
  local copies, waits for them, and re-layouts: 5.95 us -> 2.26 us
  Pallas kernels: 57 us -> 55 us
    unnamed x11 -> x1, local copies, waits for them, and re-layouts: 5.95 us -> 2.26 us
    pallas_call x1, Pallas kernels: 57 us -> 55 us  [body(): pl.pallas_call(functools.partial(kernel, n_row, n_col, minor_col), out_sh...]
where the time goes in v3:
time: 57.4 us; the launch traced here: 57.2 us
  Pallas kernels  55 us (96%)
  local copies, waits for them, and re-layouts  2.26 us (4%)
    pallas_call x1, Pallas kernels, body(): pl.pallas_call(functools.partial(kernel, n_row, n_col, minor_col), out_sh...  55 us
    unnamed x1, local copies, waits for them, and re-layouts  2.26 us

profile of v3, /device:TPU:28, one launch (start us, length us, event | category | flops | bytes accessed | tf_op | source)
XLA Modules:
  0.0 57.2 jit_solution(14050674179192073624)
XLA Ops:
  0.0 55.0 %shard_map.55 = bf16[2,2,512,256]{3,2,1,0:T(8,128)(2,1)} custom-call(s32[2,2]{1,0:T(2,128)} %ranks.1, bf16[2,2,512,256]{3,2,1,0:T(8,128)(2,1)} %left.1, bf16[2,2,512,256]{3,2,1,0:T(8,128)(2,1)} %right.1, bf16[2,128,512]{2,1,0:T(8,128)(2,1)} %lower.1, bf16[2,64,512]{2,1,0:T(8,128)(2,1)} %bitcast.1), custom_call_target="tpu_custom_call" | custom-call | flops 2000000000 | bytes 4000000 | tf_op jit(solution)/shard_map/pallas_call | solution.py:387
  55.0 2.3 %copy.7 = bf16[2,2,512,256]{3,2,1,0:T(8,128)(2,1)} copy(bf16[2,2,512,256]{3,2,1,0:T(8,128)(2,1)} %shard_map.55) | data formatting | bytes 2097152

commit v4 on v3

--- a/solution.py
+++ b/solution.py
@@ -148,8 +148,8 @@
             for chunk in range(CHUNKS):
                 forward(item, chunk)
 
-    def relay(items, also=True):
-        for chunk in range(CHUNKS):
+    def relay(items, also=True, chunks=range(CHUNKS)):
+        for chunk in chunks:
             for item, main in items:
                 role = is_main(item) if main else jnp.logical_not(is_main(item))
 
@@ -338,12 +338,19 @@
     main(("cy", 0, 1), ("cy", 1, 0), ("ru", 0, 1), ("ru", 1, 1))
     leaf(("cu", 0, 1))
     leaf(("cy", 0, 1))
-    update(0, 1, 0)
+    update(0, 1, 0, also=c == 1)
     solve_next(1)
     leaf(("ry", 0, 1), ("ru", 0, 1), also=r != 1)
+    quarter = CHUNKS // 4
+    last = [range(quarter * n, quarter * (n + 1)) for n in range(4)]
+    relay([(("cy", 1, 1), True)], chunks=last[0])
+    update(0, 1, 0, also=c != 1)
+    relay([(("cy", 1, 1), True)], chunks=last[1])
     update(0, 0, 1, also=r != 1)
+    relay([(("cy", 1, 1), True)], chunks=last[2])
     update(0, 1, 1)
-    main(("cy", 1, 1), ("ry", 1, 0))
+    relay([(("cy", 1, 1), True)], chunks=last[3])
+    main(("ry", 1, 0))
     main(("ry", 1, 1))
     leaf(("cu", 1, 0), ("cy", 1, 0), ("ru", 1, 0), ("ry", 1, 0))
     update(1, 0, 0)

time: 57.4 us -> 56.1 us (0.977)
  Pallas kernels: 55 us -> 53.6 us
    pallas_call x1, Pallas kernels: 55 us -> 53.6 us  [body(): pl.pallas_call(functools.partial(kernel, n_row, n_col, minor_col), out_sh...]
where the time goes in v4:
time: 56.1 us; the launch traced here: 55.9 us
  Pallas kernels  53.6 us (96%)
  local copies, waits for them, and re-layouts  2.26 us (4%)
    pallas_call x1, Pallas kernels, body(): pl.pallas_call(functools.partial(kernel, n_row, n_col, minor_col), out_sh...  53.6 us
    unnamed x1, local copies, waits for them, and re-layouts  2.26 us

profile of v4, /device:TPU:28, one launch (start us, length us, event | category | flops | bytes accessed | tf_op | source)
XLA Modules:
  0.0 55.9 jit_solution(14675373165151027733)
XLA Ops:
  0.0 53.6 %shard_map.55 = bf16[2,2,512,256]{3,2,1,0:T(8,128)(2,1)} custom-call(s32[2,2]{1,0:T(2,128)} %ranks.1, bf16[2,2,512,256]{3,2,1,0:T(8,128)(2,1)} %left.1, bf16[2,2,512,256]{3,2,1,0:T(8,128)(2,1)} %right.1, bf16[2,128,512]{2,1,0:T(8,128)(2,1)} %lower.1, bf16[2,64,512]{2,1,0:T(8,128)(2,1)} %bitcast.1), custom_call_target="tpu_custom_call" | custom-call | flops 2000000000 | bytes 4000000 | tf_op jit(solution)/shard_map/pallas_call | solution.py:394
  53.6 2.3 %copy.7 = bf16[2,2,512,256]{3,2,1,0:T(8,128)(2,1)} copy(bf16[2,2,512,256]{3,2,1,0:T(8,128)(2,1)} %shard_map.55) | data formatting | bytes 2097152
